TPU v7x, 32 devices: a whole 2x2x4 slice. The times are simulated.
32 devices in a mesh: dp: 4 (over x, core), sp: 8 (over z, y).
Axes of the slice: x: 2, y: 2, z: 4, core: 2. Of those that a mesh axis runs over, the one named last changes fastest.
Arguments:
- frames_in: bfloat16 [2048, 64, 256], P(('dp', 'sp')), may hold values from -6 to 6
- spatial_weight: bfloat16 [3, 3, 256, 256], replicated, may hold values from -0.125 to 0.125
- temporal_weight: bfloat16 [3, 256, 256], replicated, may hold values from -0.21875 to 0.21875
- cotangent: bfloat16 [2048, 64, 256], P(('dp', 'sp')), may hold values from -6 to 6
Outputs:
- block_out: bfloat16 [2048, 64, 256], P(('dp', 'sp'))
- grad_input: bfloat16 [2048, 64, 256], P(('dp', 'sp'))
- grad_spatial: float32 [3, 3, 256, 256], replicated
- grad_temporal: float32 [3, 256, 256], replicated
All inputs are finite; a program needn't handle non-finite values.
Results may differ from a plain program's by a relative error of at most 0.0049.
Values may be sent and summed in bfloat16 or wider, within the bound.
A program may use at most 128 MiB of HBM per device.

v0:
```python
import math
import jax
import jax.numpy as jnp
from jax import lax
from jax.sharding import PartitionSpec as P

H = 64
FRAMES = 4


def contract_rows(left, right):
    return lax.dot_general(
        left, right, (((0,), (0,)), ((), ())), preferred_element_type=jnp.float32
    )


def times_transpose(left, weight):
    return lax.dot_general(
        left, weight, (((1,), (1,)), ((), ())), preferred_element_type=jnp.float32
    )


def local(frames_in, spatial_weight, temporal_weight, cotangent):
    slab_rows, width_cells, channels = frames_in.shape
    sp_count = lax.axis_size("sp")

    def padded_rows(values):
        return jnp.pad(values, ((1, 1), (1, 1), (0, 0)))

    def flatten_rows(values):
        return values.reshape(-1, channels)

    padded_in = padded_rows(frames_in)
    pre = jnp.zeros((slab_rows * width_cells, channels), jnp.float32)
    for tap_row in range(3):
        for tap_col in range(3):
            window = flatten_rows(
                padded_in[tap_row : tap_row + slab_rows, tap_col : tap_col + width_cells]
            )
            pre = pre + jnp.dot(
                window, spatial_weight[tap_row, tap_col], preferred_element_type=jnp.float32
            )
    act = jax.nn.silu(pre).astype(jnp.bfloat16).reshape(slab_rows, width_cells, channels)

    def to_frames(values):
        return lax.all_to_all(values, "sp", split_axis=0, concat_axis=1, tiled=True)

    moved_act, moved_cot = (
        lax.all_to_all(act, "sp", split_axis=1, concat_axis=0, tiled=True),
        lax.all_to_all(cotangent, "sp", split_axis=1, concat_axis=0, tiled=True),
    )
    group_rows = slab_rows * sp_count
    stripe = width_cells // sp_count
    groups = group_rows // (FRAMES * H)
    act_clips = moved_act.reshape(groups, FRAMES, H * stripe, channels)
    cot_clips = moved_cot.reshape(groups, FRAMES, H * stripe, channels)
    act_padded = jnp.pad(act_clips, ((0, 0), (2, 0), (0, 0), (0, 0)))
    cot_padded = jnp.pad(cot_clips, ((0, 0), (0, 2), (0, 0), (0, 0)))
    temporal_sum = jnp.zeros(act_clips.shape, jnp.float32)
    act_grad_sum = jnp.zeros(act_clips.shape, jnp.float32)
    temporal_terms = []
    for tap_step in range(3):
        earlier = act_padded[:, 2 - tap_step : 2 - tap_step + FRAMES]
        temporal_sum = temporal_sum + jnp.einsum(
            "gfpc,cd->gfpd", earlier, temporal_weight[tap_step], preferred_element_type=jnp.float32
        )
        temporal_terms.append(
            jnp.einsum("gfpc,gfpd->cd", earlier, cot_clips, preferred_element_type=jnp.float32)
        )
        later = cot_padded[:, tap_step : tap_step + FRAMES]
        act_grad_sum = act_grad_sum + jnp.einsum(
            "gfpd,cd->gfpc", later, temporal_weight[tap_step], preferred_element_type=jnp.float32
        )
    temporal_out = to_frames(
        temporal_sum.astype(jnp.bfloat16).reshape(group_rows, stripe, channels)
    )
    grad_act = to_frames(act_grad_sum.astype(jnp.bfloat16).reshape(group_rows, stripe, channels))
    grad_temporal = jnp.stack(temporal_terms)
    grad_scale = 1.0 / math.sqrt(slab_rows * sp_count * lax.axis_size("dp") * width_cells)
    block_out = (frames_in.astype(jnp.float32) + temporal_out.astype(jnp.float32)).astype(
        jnp.bfloat16
    )
    sigma = jax.nn.sigmoid(pre)
    grad_pre = (
        flatten_rows(grad_act).astype(jnp.float32) * (sigma * (1.0 + pre * (1.0 - sigma)))
    ).astype(jnp.bfloat16)
    grad_padded = padded_rows(grad_pre.reshape(slab_rows, width_cells, channels))
    spatial_terms = []
    grad_in = flatten_rows(cotangent).astype(jnp.float32)
    for tap_row in range(3):
        for tap_col in range(3):
            window = flatten_rows(
                padded_in[tap_row : tap_row + slab_rows, tap_col : tap_col + width_cells]
            )
            spatial_terms.append(contract_rows(window, grad_pre))
            back_window = flatten_rows(
                grad_padded[
                    2 - tap_row : 2 - tap_row + slab_rows, 2 - tap_col : 2 - tap_col + width_cells
                ]
            )
            grad_in = grad_in + times_transpose(back_window, spatial_weight[tap_row, tap_col])
    grad_spatial = jnp.stack(spatial_terms).reshape(3, 3, channels, channels)
    grad_spatial, grad_temporal = lax.psum((grad_spatial, grad_temporal), ("dp", "sp"))
    grad_input = grad_in.astype(jnp.bfloat16).reshape(slab_rows, width_cells, channels)
    return (block_out, grad_input, grad_spatial * grad_scale, grad_temporal * grad_scale)


def solution(mesh):
    placed = (P(("dp", "sp"), None, None), P(), P(), P(("dp", "sp"), None, None))
    return jax.shard_map(
        local,
        mesh=mesh,
        in_specs=placed,
        out_specs=(P(("dp", "sp"), None, None), P(("dp", "sp"), None, None), P(), P()),
        check_vma=False,
    )
```

profile of v0, /device:TPU:0, one launch (start us, length us, event | category | flops | bytes accessed | tf_op | source)
XLA Modules:
  0.0 385.7 jit_solution(17746489602125472998)
XLA Ops:
  7.2 4.1 %copy.32 = bf16[64,64,256]{2,0,1:T(8,128)(2,1)} copy(bf16[64,64,256]{2,1,0:T(8,128)(2,1)} %param.7) | data formatting | bytes 4194304 | tf_op args[3]
  11.3 7.4 %all-to-all-start.2 = ((bf16[64,64,256]{2,0,1:T(8,128)(2,1)}), bf16[64,64,256]{2,0,1:T(8,128)(2,1)}, u32[]{:S(2)}, u32[]{:S(2)}) async-start(bf16[64,64,256]{2,0,1:T(8,128)(2,1)} %copy.32), calls=%async_computation.2 | async-start | bytes 4194304 | tf_op jit(solution)/shard_map/all_to_all | solution.py:50
  18.7 9.8 %pad_slice_fusion.10 = (bf16[64,64,256]{2,1,0:T(8,128)(2,1)}, bf16[64,64,256]{2,1,0:T(8,128)(2,1)}, bf16[64,64,256]{2,1,0:T(8,128)(2,1)}, bf16[64,64,256]{2,1,0:...) fusion(bf16[64,64,256]{2,1,0:T(8,128)(2,1)S(1)} %copy-done.3), kind=kLoop, calls=%fused_computation.46 | loop fusion | bytes 18874368 | tf_op jit(solution)/shard_map/slice | solution.py:38
  28.4 38.6 %all-to-all-done.2 = bf16[64,64,256]{2,0,1:T(8,128)(2,1)} async-done(((bf16[64,64,256]{2,0,1:T(8,128)(2,1)}), bf16[64,64,256]{2,0,1:T(8,128)(2,1)}, u32[]{:S(2)}, u32[]{:S(2)}) %all-to-all-start.2) | async-done | bytes 2097184 | tf_op jit(solution)/shard_map/all_to_all | solution.py:50
  67.0 2.9 copy.33
  71.4 2.1 add_convert_fusion
  73.5 4.8 %all-to-all-start.3 = ((bf16[512,8,256]{2,1,0:T(8,128)(2,1)}), bf16[512,8,256]{2,1,0:T(8,128)(2,1)}, u32[]{:S(2)}, u32[]{:S(2)}) async-start(bf16[512,8,256]{2,1,0:T(8,128)(2,1)} %bitcast.239), calls=%async_computation.3 | async-start | bytes 4194304 | tf_op jit(solution)/shard_map/all_to_all | solution.py:46
  78.3 2.4 fusion.63
  81.5 0.9 copy-done.16
  83.1 0.9 copy-done.13
  84.7 0.8 convolution_add_fusion.13
  85.5 0.8 copy-done.10
  87.0 0.9 copy-done.8
  88.6 0.9 copy-done.6
  89.4 2.7 convolution_add_fusion.10
  92.1 34.0 %all-to-all-done.3 = bf16[512,8,256]{2,1,0:T(8,128)(2,1)} async-done(((bf16[512,8,256]{2,1,0:T(8,128)(2,1)}), bf16[512,8,256]{2,1,0:T(8,128)(2,1)}, u32[]{:S(2)}, u32[]{:S(2)}) %all-to-all-start.3) | async-done | bytes 2097184 | tf_op jit(solution)/shard_map/all_to_all | solution.py:46
  126.1 2.0 convert_bitcast_fusion
  128.7 1.6 copy-done.23
  130.9 3.5 fusion.2
  134.4 2.5 copy.29
  137.0 4.9 %all-to-all-start = ((bf16[64,64,256]{2,0,1:T(8,128)(2,1)}), bf16[64,64,256]{2,0,1:T(8,128)(2,1)}, u32[]{:S(2)}, u32[]{:S(2)}) async-start(bf16[64,64,256]{2,0,1:T(8,128)(2,1)} %copy.29), calls=%async_computation | async-start | bytes 4194304 | tf_op jit(solution)/shard_map/all_to_all | solution.py:49
  141.9 3.1 fusion.35
  145.3 0.8 fusion.34
  146.1 0.8 copy-done.17
  146.9 0.8 fusion.33
  147.7 0.8 copy-done.14
  149.3 1.0 fusion.31
  151.7 0.8 copy-done.9
  153.3 0.8 copy-done.7
  154.9 0.8 copy-done.26
  156.4 1.4 copy-done.24
  157.8 10.4 %pad_slice_fusion.2 = (bf16[64,64,256]{2,1,0:T(8,128)(2,1)}, bf16[64,64,256]{2,1,0:T(8,128)(2,1)S(1)}, bf16[64,64,256]{2,1,0:T(8,128)(2,1)S(1)}, bf16[64,64,256]...) fusion(bf16[64,64,256]{2,1,0:T(8,128)(2,1)S(1)} %bitcast.256), kind=kLoop, calls=%fused_computation.38 | loop fusion | bytes 18874368 | tf_op jit(solution)/shard_map/slice | solution.py:97
  168.3 0.8 convolution_add_fusion.8
  171.3 2.8 convolution_add_fusion.4
  174.1 15.5 %all-to-all-done = bf16[64,64,256]{2,0,1:T(8,128)(2,1)} async-done(((bf16[64,64,256]{2,0,1:T(8,128)(2,1)}), bf16[64,64,256]{2,0,1:T(8,128)(2,1)}, u32[]{:S(2)}, u32[]{:S(2)}) %all-to-all-start) | async-done | bytes 2097184 | tf_op jit(solution)/shard_map/all_to_all | solution.py:49
  189.6 3.0 copy.30
  195.1 2.0 add_convert_fusion.1
  197.1 4.4 %all-to-all-start.1 = ((bf16[512,8,256]{2,1,0:T(8,128)(2,1)}), bf16[512,8,256]{2,1,0:T(8,128)(2,1)}, u32[]{:S(2)}, u32[]{:S(2)}) async-start(bf16[512,8,256]{2,1,0:T(8,128)(2,1)} %bitcast.238), calls=%async_computation.1 | async-start | bytes 4194304 | tf_op jit(solution)/shard_map/all_to_all | solution.py:46
  202.0 1.3 copy-done.2
  204.8 0.9 pad_maximum_fusion
  205.8 3.7 convolution_add_fusion.3
  209.5 0.8 convolution_add_fusion.2
  211.8 0.8 copy-done.12
  212.7 2.1 fusion
  214.8 154.8 %all-reduce.7.cloned.1.call-done = (f32[3,3,256,256]{3,2,1,0:T(8,128)}, f32[3,256,256]{2,1,0:T(8,128)}) async-done(((f32[3,3,256,256]{3,2,1,0:T(8,128)}, f32[3,256,256]{2,1,0:T(8,128)}), (f32[3,3,256,256]{3,2,1,0:T(8,128)}, f32[3,256,256]{2,1,0:T(8,128)})) %all-reduce.7.cloned.1.call-update) | async-done | bytes 3145744 | tf_op jit(solution)/shard_map/psum | solution.py:103
  369.6 2.1 broadcast_multiply_fusion.1
  371.6 3.4 broadcast_multiply_fusion
  375.1 3.6 fusion.1
  (70 shorter events, 19.3 us)
Async XLA Ops:
  11.2 7.4 %copy-start.3 = (bf16[64,64,256]{2,1,0:T(8,128)(2,1)S(1)}, bf16[64,64,256]{2,1,0:T(8,128)(2,1)}, u32[]{:S(2)}) copy-start(bf16[64,64,256]{2,1,0:T(8,128)(2,1)} %param.4) | copy-start | bytes 6291460
  11.3 55.8 %all-to-all-start.2 = ((bf16[64,64,256]{2,0,1:T(8,128)(2,1)}), bf16[64,64,256]{2,0,1:T(8,128)(2,1)}, u32[]{:S(2)}, u32[]{:S(2)}) async-start(bf16[64,64,256]{2,0,1:T(8,128)(2,1)} %copy.32), calls=%async_computation.2 | async-start | bytes 4194304 | tf_op jit(solution)/shard_map/all_to_all | solution.py:50
  67.0 2.9 copy-start.27
  69.9 1.5 copy-start
  73.5 4.8 %copy-start.22 = (bf16[3,3,256,256]{3,2,1,0:T(8,128)(2,1)S(1)}, bf16[3,3,256,256]{3,2,1,0:T(8,128)(2,1)}, u32[]{:S(2)}) copy-start(bf16[3,3,256,256]{3,2,1,0:T(8,128)(2,1)} %param.5) | copy-start | bytes 3538948
  73.5 52.6 %all-to-all-start.3 = ((bf16[512,8,256]{2,1,0:T(8,128)(2,1)}), bf16[512,8,256]{2,1,0:T(8,128)(2,1)}, u32[]{:S(2)}, u32[]{:S(2)}) async-start(bf16[512,8,256]{2,1,0:T(8,128)(2,1)} %bitcast.239), calls=%async_computation.3 | async-start | bytes 4194304 | tf_op jit(solution)/shard_map/all_to_all | solution.py:46
  78.3 2.5 copy-start.19
  80.8 1.6 copy-start.16
  82.4 1.6 copy-start.13
  84.7 1.6 copy-start.10
  86.3 1.6 copy-start.8
  87.8 1.6 copy-start.6
  128.1 2.2 copy-start.23
  128.1 2.9 copy-start.25
  137.0 52.7 %all-to-all-start = ((bf16[64,64,256]{2,0,1:T(8,128)(2,1)}), bf16[64,64,256]{2,0,1:T(8,128)(2,1)}, u32[]{:S(2)}, u32[]{:S(2)}) async-start(bf16[64,64,256]{2,0,1:T(8,128)(2,1)} %copy.29), calls=%async_computation | async-start | bytes 4194304 | tf_op jit(solution)/shard_map/all_to_all | solution.py:49
  141.9 3.1 copy-start.20
  141.9 3.5 copy-start.21
  145.3 1.6 copy-start.17
  146.9 1.6 copy-start.14
  149.3 1.6 copy-start.11
  150.9 1.6 copy-start.9
  152.5 1.6 copy-start.7
  154.1 1.6 copy-start.26
  156.4 1.4 copy-start.24
  157.8 10.5 %copy-start.5 = (bf16[64,64,256]{2,1,0:T(8,128)(2,1)S(1)}, bf16[64,64,256]{2,1,0:T(8,128)(2,1)}, u32[]{:S(2)}) copy-start(bf16[64,64,256]{2,1,0:T(8,128)(2,1)} %param.7) | copy-start | bytes 6291460
  189.6 3.0 copy-start.1
  192.7 1.0 copy-start.28
  197.1 178.0 %all-to-all-start.1 = ((bf16[512,8,256]{2,1,0:T(8,128)(2,1)}), bf16[512,8,256]{2,1,0:T(8,128)(2,1)}, u32[]{:S(2)}, u32[]{:S(2)}) async-start(bf16[512,8,256]{2,1,0:T(8,128)(2,1)} %bitcast.238), calls=%async_computation.1 | async-start | bytes 4194304 | tf_op jit(solution)/shard_map/all_to_all | solution.py:46
  201.5 168.1 %all-reduce.7.cloned.1.call-start = ((), (), s32[]{:S(2)}) async-start(), calls=%async_computation.4 | async-start | bytes 6291456 | tf_op jit(solution)/shard_map/psum | solution.py:103
  201.7 1.6 copy-start.2
  205.8 3.7 copy-start.18
  209.5 1.6 copy-start.15
  211.1 1.6 copy-start.12
  371.6 3.4 copy-start.4
Sparse Core Ops, SparseCore 0:
  208.5 160.9 all-reduce.6
where the time goes:
time: 393 us; the launch traced here: 386 us
  waiting for transfers between devices  243 us (62%)
  local copies, waits for them, and re-layouts  49.7 us (13%)
  matrix products  44.8 us (11%)
  starting transfers between devices  21.7 us (6%)
  between operations  14.7 us (4%)
  other arithmetic  12 us (3%)
    psum x1, waiting for transfers between devices, local(): lax.psum((grad_spatial, grad_temporal), ('dp', 'sp'))  155 us
    all_to_all x1, waiting for transfers between devices, local(): lax.all_to_all(cotangent, 'sp', split_axis=1, concat_axis=0, tiled=True)  38.6 us
    all_to_all x2, waiting for transfers between devices, to_frames(): return lax.all_to_all(values, 'sp', split_axis=0, concat_axis=1, tiled=True)  34 us
    unnamed x59, local copies, waits for them, and re-layouts  20.2 us
    all_to_all x1, waiting for transfers between devices, local(): lax.all_to_all(act, 'sp', split_axis=1, concat_axis=0, tiled=True)  15.5 us
    dot_general x9, matrix products, times_transpose(): lax.dot_general(left, weight, (((1,), (1,)), ((), ())), preferred_element...  13.1 us
    dot_general x9, matrix products, local(): jnp.dot(window, spatial_weight[tap_row, tap_col], preferred_element_type=...  13 us
    slice x1, local copies, waits for them, and re-layouts, local(): grad_padded[2 - tap_row:2 - tap_row + slab_rows, 2 - tap_col:2 - tap_col...  10.4 us
  transfers between devices with their start and end apart: 5, of which 4 were waited for; matrix products, arithmetic and copies ran while one was open for 16% of the time, Pallas kernels for 0%

commit v1 on v0

--- a/solution.py
+++ b/solution.py
@@ -21,6 +21,24 @@
 
 
 def local(frames_in, spatial_weight, temporal_weight, cotangent):
+
+    def register_rails(u):
+        last, y_new = (lax.axis_size("sp"), lax.axis_index("sp"))
+        x_now = u.shape[1] // last
+        z_new = list(u.shape)
+        z_new[1] = x_now
+        everything = z_new[0]
+        z_new[0] = everything * last
+        mid_arr = jnp.zeros(z_new, u.dtype)
+        for hop_no in range(last):
+            t_next = lax.dynamic_slice_in_dim(u, (y_new ^ hop_no) * x_now, x_now, axis=1)
+            if hop_no:
+                t_next = lax.ppermute(t_next, "sp", [(c, c ^ hop_no) for c in range(last)])
+            mid_arr = lax.dynamic_update_slice_in_dim(
+                mid_arr, t_next, (y_new ^ hop_no) * everything, axis=0
+            )
+        return mid_arr
+
     slab_rows, width_cells, channels = frames_in.shape
     sp_count = lax.axis_size("sp")
 
@@ -47,7 +65,7 @@
 
     moved_act, moved_cot = (
         lax.all_to_all(act, "sp", split_axis=1, concat_axis=0, tiled=True),
-        lax.all_to_all(cotangent, "sp", split_axis=1, concat_axis=0, tiled=True),
+        register_rails(cotangent),
     )
     group_rows = slab_rows * sp_count
     stripe = width_cells // sp_count

time: 393 us -> 386 us (0.982)
  waiting for transfers between devices: 243 us -> 221 us
  starting transfers between devices: 21.7 us -> 36.5 us
    all_to_all x1 -> x0, waiting for transfers between devices: 38.6 us -> none  [local(): lax.all_to_all(cotangent, 'sp', split_axis=1, concat_axis=0, tiled=True)]
    ppermute x0 -> x7, starting transfers between devices: none -> 21 us  [register_rails(): t_next = lax.ppermute(t_next, 'sp', [(c, c ^ hop_no) for c in range(last)])]
    ppermute x0 -> x7, waiting for transfers between devices: none -> 17.5 us  [register_rails(): t_next = lax.ppermute(t_next, 'sp', [(c, c ^ hop_no) for c in range(last)])]
    all_to_all x1 -> x0, starting transfers between devices: 7.41 us -> none  [local(): lax.all_to_all(cotangent, 'sp', split_axis=1, concat_axis=0, tiled=True)]
    dynamic_update_slice x0 -> x7, local copies, waits for them, and re-layouts: none -> 4.9 us  [register_rails(): lax.dynamic_update_slice_in_dim(mid_arr, t_next, (y_new ^ hop_no) * every...]
    unnamed x59 -> x66, local copies, waits for them, and re-layouts: 20.2 us -> 20.3 us
  transfers between devices with their start and end apart: 5 -> 11, of which waited for: 4 -> 5; matrix products, arithmetic and copies ran while one was open for 16% -> 16% of each run, Pallas kernels for 0% -> 0%
where the time goes in v1:
time: 386 us; the launch traced here: 380 us
  waiting for transfers between devices  221 us (57%)
  local copies, waits for them, and re-layouts  53 us (14%)
  matrix products  42.2 us (11%)
  starting transfers between devices  36.5 us (9%)
  between operations  14.8 us (4%)
  other arithmetic  11.9 us (3%)
    psum x1, waiting for transfers between devices, local(): lax.psum((grad_spatial, grad_temporal), ('dp', 'sp'))  154 us
    all_to_all x2, waiting for transfers between devices, to_frames(): return lax.all_to_all(values, 'sp', split_axis=0, concat_axis=1, tiled=True)  33.7 us
    ppermute x7, starting transfers between devices, register_rails(): t_next = lax.ppermute(t_next, 'sp', [(c, c ^ hop_no) for c in range(last)])  21 us
    unnamed x66, local copies, waits for them, and re-layouts  20.3 us
    ppermute x7, waiting for transfers between devices, register_rails(): t_next = lax.ppermute(t_next, 'sp', [(c, c ^ hop_no) for c in range(last)])  17.5 us
    all_to_all x1, waiting for transfers between devices, local(): lax.all_to_all(act, 'sp', split_axis=1, concat_axis=0, tiled=True)  15.6 us
    dot_general x9, matrix products, times_transpose(): lax.dot_general(left, weight, (((1,), (1,)), ((), ())), preferred_element...  12.4 us
    dot_general x9, matrix products, local(): jnp.dot(window, spatial_weight[tap_row, tap_col], preferred_element_type=...  11.1 us
  transfers between devices with their start and end apart: 11, of which 5 were waited for; matrix products, arithmetic and copies ran while one was open for 16% of the time, Pallas kernels for 0%

profile of v1, /device:TPU:0, one launch (start us, length us, event | category | flops | bytes accessed | tf_op | source)
XLA Modules:
  0.0 379.5 jit_solution(8084926303365813939)
XLA Ops:
  7.4 1.4 copy-done.6
  8.8 1.1 constant_dynamic-slice_fusion
  9.9 6.0 %collective-permute-start.6 = (bf16[64,8,256]{2,1,0:T(8,128)(2,1)S(1)}, bf16[64,8,256]{2,1,0:T(8,128)(2,1)}, u32[]{:S(2)}, u32[]{:S(2)}) collective-permute-start(bf16[64,8,256]{2,1,0:T(8,128)(2,1)S(1)} %get-tuple-element.18), channel_id=1, source_target_pairs={{0,7},{1,6},{2,5},{3,4},{4,3},{5,2},{6,1},{7,0},{8,15},{9,14},{10,... | collective-permute-start | bytes 786440 | tf_op jit(solution)/shard_map/ppermute | solution.py:36
  15.9 1.7 collective-permute-start.2
  18.2 1.1 collective-permute-start
  19.4 9.8 %pad_slice_fusion.10 = (bf16[64,64,256]{2,1,0:T(8,128)(2,1)}, bf16[64,64,256]{2,1,0:T(8,128)(2,1)}, bf16[64,64,256]{2,1,0:T(8,128)(2,1)}, bf16[64,64,256]{2,1,0:...) fusion(bf16[64,64,256]{2,1,0:T(8,128)(2,1)S(1)} %copy-done.3), kind=kLoop, calls=%fused_computation.46 | loop fusion | bytes 18874368 | tf_op jit(solution)/shard_map/slice | solution.py:56
  29.2 4.5 %collective-permute-done = bf16[64,8,256]{2,1,0:T(8,128)(2,1)} collective-permute-done((bf16[64,8,256]{2,1,0:T(8,128)(2,1)}, bf16[64,8,256]{2,1,0:T(8,128)(2,1)}, u32[]{:S(2)}, u32[]{:S(2)}) %collective-permute-start) | collective-permute-done | bytes 262176 | tf_op jit(solution)/shard_map/ppermute | solution.py:36
  33.6 10.1 %collective-permute-start.3 = (bf16[64,8,256]{2,1,0:T(8,128)(2,1)S(1)}, bf16[64,8,256]{2,1,0:T(8,128)(2,1)S(1)}, u32[]{:S(2)}, u32[]{:S(2)}) collective-permute-start(bf16[64,8,256]{2,1,0:T(8,128)(2,1)S(1)} %get-tuple-element.20), channel_id=1, source_target_pairs={{0,4},{1,5},{2,6},{3,7},{4,0},{5,1},{6,2},{7,3},{8,12},{9,13},{10,... | collective-permute-start | bytes 786440 | tf_op jit(solution)/shard_map/ppermute | solution.py:36
  43.8 1.0 constant_dynamic-update-slice_fusion.5
  44.7 1.3 collective-permute-start.5
  46.1 1.0 constant_dynamic-update-slice_fusion.4
  47.1 1.0 constant_dynamic-update-slice_fusion.3
  48.0 13.1 %collective-permute-done.3 = bf16[64,8,256]{2,1,0:T(8,128)(2,1)S(1)} collective-permute-done((bf16[64,8,256]{2,1,0:T(8,128)(2,1)S(1)}, bf16[64,8,256]{2,1,0:T(8,128)(2,1)S(1)}, u32[]{:S(2)}, u32[]{:S(2)}) %collective-permute-start.3) | collective-permute-done | bytes 262176 | tf_op jit(solution)/shard_map/ppermute | solution.py:36
  61.1 1.0 constant_dynamic-update-slice_fusion.1
  62.2 1.0 constant_dynamic-update-slice_fusion.6
  64.7 2.1 add_convert_fusion
  66.7 6.0 %all-to-all-start.2 = ((bf16[512,8,256]{2,1,0:T(8,128)(2,1)}), bf16[512,8,256]{2,1,0:T(8,128)(2,1)}, u32[]{:S(2)}, u32[]{:S(2)}) async-start(bf16[512,8,256]{2,1,0:T(8,128)(2,1)} %bitcast.238), calls=%async_computation.2 | async-start | bytes 4194304 | tf_op jit(solution)/shard_map/all_to_all | solution.py:64
  73.5 0.9 copy-done.19
  75.1 0.9 copy-done.17
  76.7 0.9 copy-done.15
  78.3 0.9 copy-done.4
  81.5 0.9 copy-done.11
  83.1 0.9 copy-done.9
  83.9 2.7 convolution_add_fusion.10
  86.6 33.7 %all-to-all-done.2 = bf16[512,8,256]{2,1,0:T(8,128)(2,1)} async-done(((bf16[512,8,256]{2,1,0:T(8,128)(2,1)}), bf16[512,8,256]{2,1,0:T(8,128)(2,1)}, u32[]{:S(2)}, u32[]{:S(2)}) %all-to-all-start.2) | async-done | bytes 2097184 | tf_op jit(solution)/shard_map/all_to_all | solution.py:64
  120.3 2.0 convert_bitcast_fusion
  122.9 1.6 copy-done.27
  125.2 3.5 fusion.2
  128.6 2.5 copy.27
  131.1 4.9 %all-to-all-start = ((bf16[64,64,256]{2,0,1:T(8,128)(2,1)}), bf16[64,64,256]{2,0,1:T(8,128)(2,1)}, u32[]{:S(2)}, u32[]{:S(2)}) async-start(bf16[64,64,256]{2,0,1:T(8,128)(2,1)} %copy.27), calls=%async_computation | async-start | bytes 4194304 | tf_op jit(solution)/shard_map/all_to_all | solution.py:67
  136.1 3.1 fusion.35
  143.5 1.0 fusion.31
  150.6 1.4 copy-done.28
  152.0 10.4 %pad_slice_fusion.2 = (bf16[64,64,256]{2,1,0:T(8,128)(2,1)}, bf16[64,64,256]{2,1,0:T(8,128)(2,1)S(1)}, bf16[64,64,256]{2,1,0:T(8,128)(2,1)S(1)}, bf16[64,64,256]...) fusion(bf16[64,64,256]{2,1,0:T(8,128)(2,1)S(1)} %bitcast.255), kind=kLoop, calls=%fused_computation.38 | loop fusion | bytes 18874368 | tf_op jit(solution)/shard_map/slice | solution.py:115
  165.5 2.8 convolution_add_fusion.4
  168.3 15.6 %all-to-all-done = bf16[64,64,256]{2,0,1:T(8,128)(2,1)} async-done(((bf16[64,64,256]{2,0,1:T(8,128)(2,1)}), bf16[64,64,256]{2,0,1:T(8,128)(2,1)}, u32[]{:S(2)}, u32[]{:S(2)}) %all-to-all-start) | async-done | bytes 2097184 | tf_op jit(solution)/shard_map/all_to_all | solution.py:67
  183.9 3.0 copy.28
  189.3 2.0 add_convert_fusion.1
  191.3 4.4 %all-to-all-start.1 = ((bf16[512,8,256]{2,1,0:T(8,128)(2,1)}), bf16[512,8,256]{2,1,0:T(8,128)(2,1)}, u32[]{:S(2)}, u32[]{:S(2)}) async-start(bf16[512,8,256]{2,1,0:T(8,128)(2,1)} %bitcast.237), calls=%async_computation.1 | async-start | bytes 4194304 | tf_op jit(solution)/shard_map/all_to_all | solution.py:64
  196.3 1.3 copy-done.2
  199.0 0.9 pad_maximum_fusion
  200.0 0.9 copy-done.24
  200.9 3.1 convolution_add_fusion.3
  207.2 2.1 fusion
  209.2 154.2 %all-reduce.7.cloned.1.call-done = (f32[3,3,256,256]{3,2,1,0:T(8,128)}, f32[3,256,256]{2,1,0:T(8,128)}) async-done(((f32[3,3,256,256]{3,2,1,0:T(8,128)}, f32[3,256,256]{2,1,0:T(8,128)}), (f32[3,3,256,256]{3,2,1,0:T(8,128)}, f32[3,256,256]{2,1,0:T(8,128)})) %all-reduce.7.cloned.1.call-update) | async-done | bytes 3145744 | tf_op jit(solution)/shard_map/psum | solution.py:121
  363.5 2.1 broadcast_multiply_fusion.1
  365.5 3.4 broadcast_multiply_fusion
  369.0 3.5 fusion.1
  (97 shorter events, 30.4 us)
Async XLA Ops:
  7.2 1.6 copy-start.6
  8.8 10.6 %copy-start.3 = (bf16[64,64,256]{2,1,0:T(8,128)(2,1)S(1)}, bf16[64,64,256]{2,1,0:T(8,128)(2,1)}, u32[]{:S(2)}) copy-start(bf16[64,64,256]{2,1,0:T(8,128)(2,1)} %param.4) | copy-start | bytes 6291460
  9.9 52.3 %collective-permute-start.6 = (bf16[64,8,256]{2,1,0:T(8,128)(2,1)S(1)}, bf16[64,8,256]{2,1,0:T(8,128)(2,1)}, u32[]{:S(2)}, u32[]{:S(2)}) collective-permute-start(bf16[64,8,256]{2,1,0:T(8,128)(2,1)S(1)} %get-tuple-element.18), channel_id=1, source_target_pairs={{0,7},{1,6},{2,5},{3,4},{4,3},{5,2},{6,1},{7,0},{8,15},{9,14},{10,... | collective-permute-start | bytes 786440 | tf_op jit(solution)/shard_map/ppermute | solution.py:36
  15.9 45.3 %collective-permute-start.4 = (bf16[64,8,256]{2,1,0:T(8,128)(2,1)S(1)}, bf16[64,8,256]{2,1,0:T(8,128)(2,1)}, u32[]{:S(2)}, u32[]{:S(2)}) collective-permute-start(bf16[64,8,256]{2,1,0:T(8,128)(2,1)S(1)} %get-tuple-element.19), channel_id=1, source_target_pairs={{0,5},{1,4},{2,7},{3,6},{4,1},{5,0},{6,3},{7,2},{8,13},{9,12},{10,... | collective-permute-start | bytes 786440 | tf_op jit(solution)/shard_map/ppermute | solution.py:36
  15.9 31.2 %collective-permute-start.2 = (bf16[64,8,256]{2,1,0:T(8,128)(2,1)}, bf16[64,8,256]{2,1,0:T(8,128)(2,1)}, u32[]{:S(2)}, u32[]{:S(2)}) collective-permute-start(bf16[64,8,256]{2,1,0:T(8,128)(2,1)} %get-tuple-element.21), channel_id=1, source_target_pairs={{0,3},{1,2},{2,1},{3,0},{4,7},{5,6},{6,5},{7,4},{8,11},{9,10},{10,... | collective-permute-start | bytes 786440 | tf_op jit(solution)/shard_map/ppermute | solution.py:36
  17.6 27.2 %collective-permute-start.1 = (bf16[64,8,256]{2,1,0:T(8,128)(2,1)}, bf16[64,8,256]{2,1,0:T(8,128)(2,1)}, u32[]{:S(2)}, u32[]{:S(2)}) collective-permute-start(bf16[64,8,256]{2,1,0:T(8,128)(2,1)} %get-tuple-element.22), channel_id=1, source_target_pairs={{0,2},{1,3},{2,0},{3,1},{4,6},{5,7},{6,4},{7,5},{8,10},{9,11},{10,... | collective-permute-start | bytes 786440 | tf_op jit(solution)/shard_map/ppermute | solution.py:36
  18.2 15.4 %collective-permute-start = (bf16[64,8,256]{2,1,0:T(8,128)(2,1)}, bf16[64,8,256]{2,1,0:T(8,128)(2,1)}, u32[]{:S(2)}, u32[]{:S(2)}) collective-permute-start(bf16[64,8,256]{2,1,0:T(8,128)(2,1)} %get-tuple-element.23), channel_id=1, source_target_pairs={{0,1},{1,0},{2,3},{3,2},{4,5},{5,4},{6,7},{7,6},{8,9},{9,8},{10,11... | collective-permute-start | bytes 786440 | tf_op jit(solution)/shard_map/ppermute | solution.py:36
  29.2 34.0 %copy-start.31 = (bf16[3,256,256]{2,1,0:T(8,128)(2,1)S(1)}, bf16[3,256,256]{2,1,0:T(8,128)(2,1)}, u32[]{:S(2)}) copy-start(bf16[3,256,256]{2,1,0:T(8,128)(2,1)} %param.6) | copy-start | bytes 1179652
  33.6 27.5 %collective-permute-start.3 = (bf16[64,8,256]{2,1,0:T(8,128)(2,1)S(1)}, bf16[64,8,256]{2,1,0:T(8,128)(2,1)S(1)}, u32[]{:S(2)}, u32[]{:S(2)}) collective-permute-start(bf16[64,8,256]{2,1,0:T(8,128)(2,1)S(1)} %get-tuple-element.20), channel_id=1, source_target_pairs={{0,4},{1,5},{2,6},{3,7},{4,0},{5,1},{6,2},{7,3},{8,12},{9,13},{10,... | collective-permute-start | bytes 786440 | tf_op jit(solution)/shard_map/ppermute | solution.py:36
  44.7 17.4 %collective-permute-start.5 = (bf16[64,8,256]{2,1,0:T(8,128)(2,1)S(1)}, bf16[64,8,256]{2,1,0:T(8,128)(2,1)S(1)}, u32[]{:S(2)}, u32[]{:S(2)}) collective-permute-start(bf16[64,8,256]{2,1,0:T(8,128)(2,1)S(1)} %get-tuple-element.25), channel_id=1, source_target_pairs={{0,6},{1,7},{2,4},{3,5},{4,2},{5,3},{6,0},{7,1},{8,14},{9,15},{10,... | collective-permute-start | bytes 786440 | tf_op jit(solution)/shard_map/ppermute | solution.py:36
  63.1 1.5 copy-start
  66.7 6.1 %copy-start.8 = (bf16[64,64,256]{2,1,0:T(8,128)(2,1)S(1)}, bf16[64,64,256]{2,1,0:T(8,128)(2,1)}, u32[]{:S(2)}) copy-start(bf16[64,64,256]{2,1,0:T(8,128)(2,1)} %get-tuple-element.33) | copy-start | bytes 6291460
  66.7 6.1 %copy-start.26 = (bf16[3,3,256,256]{3,2,1,0:T(8,128)(2,1)S(1)}, bf16[3,3,256,256]{3,2,1,0:T(8,128)(2,1)}, u32[]{:S(2)}) copy-start(bf16[3,3,256,256]{3,2,1,0:T(8,128)(2,1)} %param.5) | copy-start | bytes 3538948
  66.7 53.6 %all-to-all-start.2 = ((bf16[512,8,256]{2,1,0:T(8,128)(2,1)}), bf16[512,8,256]{2,1,0:T(8,128)(2,1)}, u32[]{:S(2)}, u32[]{:S(2)}) async-start(bf16[512,8,256]{2,1,0:T(8,128)(2,1)} %bitcast.238), calls=%async_computation.2 | async-start | bytes 4194304 | tf_op jit(solution)/shard_map/all_to_all | solution.py:64
  72.8 1.6 copy-start.19
  74.4 1.6 copy-start.17
  76.0 1.6 copy-start.15
  77.6 1.6 copy-start.4
  79.2 1.6 copy-start.13
  80.8 1.6 copy-start.11
  82.3 1.6 copy-start.9
  122.3 2.2 copy-start.27
  122.3 2.9 copy-start.29
  131.1 52.7 %all-to-all-start = ((bf16[64,64,256]{2,0,1:T(8,128)(2,1)}), bf16[64,64,256]{2,0,1:T(8,128)(2,1)}, u32[]{:S(2)}, u32[]{:S(2)}) async-start(bf16[64,64,256]{2,0,1:T(8,128)(2,1)} %copy.27), calls=%async_computation | async-start | bytes 4194304 | tf_op jit(solution)/shard_map/all_to_all | solution.py:67
  136.0 3.1 copy-start.20
  136.1 3.5 copy-start.25
  139.5 1.6 copy-start.18
  141.1 1.6 copy-start.16
  143.5 1.6 copy-start.14
  145.1 1.6 copy-start.12
  146.7 1.6 copy-start.10
  148.3 1.6 copy-start.30
  150.6 1.4 copy-start.28
  152.0 10.4 %copy-start.7 = (bf16[64,64,256]{2,1,0:T(8,128)(2,1)S(1)}, bf16[64,64,256]{2,1,0:T(8,128)(2,1)}, u32[]{:S(2)}) copy-start(bf16[64,64,256]{2,1,0:T(8,128)(2,1)} %param.7) | copy-start | bytes 6291460
  183.9 3.0 copy-start.1
  186.9 1.0 copy-start.32
  191.3 177.6 %all-to-all-start.1 = ((bf16[512,8,256]{2,1,0:T(8,128)(2,1)}), bf16[512,8,256]{2,1,0:T(8,128)(2,1)}, u32[]{:S(2)}, u32[]{:S(2)}) async-start(bf16[512,8,256]{2,1,0:T(8,128)(2,1)} %bitcast.237), calls=%async_computation.1 | async-start | bytes 4194304 | tf_op jit(solution)/shard_map/all_to_all | solution.py:64
  195.7 167.8 %all-reduce.7.cloned.1.call-start = ((), (), s32[]{:S(2)}) async-start(), calls=%async_computation.3 | async-start | bytes 6291456 | tf_op jit(solution)/shard_map/psum | solution.py:121
  195.9 1.6 copy-start.2
  199.0 1.9 copy-start.24
  200.9 3.1 copy-start.23
  204.0 1.6 copy-start.22
  205.6 1.6 copy-start.21
  365.5 3.4 copy-start.5
Sparse Core Ops, SparseCore 0:
  202.7 160.6 all-reduce.6
